TPU v7x, 256 devices: a whole 4x4x8 slice. The times are simulated.
256 devices in a mesh: dp: 16 (over z, y_hi), seq: 8 (over x, core), mp: 2 (over y_lo).
Axes of the slice: x: 4, y: 4 (y_hi: 2, y_lo: 2; y = y_hi * 2 + y_lo), z: 8, core: 2. Of those that a mesh axis runs over, the one named last changes fastest.
Arguments:
- query: bfloat16 [16, 2048, 4096], P('dp', 'seq', 'mp'), may hold values from -60 to 60
- latents: bfloat16 [16, 48, 64, 1280], P('dp', ('seq', 'mp')), may hold values from -6 to 6
- image_slot: int32 [16, 16], P('dp'), may hold values from 0 to 47, as said below
- block_image: int32 [16, 64], P('dp'), may hold values from 0 to 15, as said below
- key_weight: bfloat16 [1280, 2, 2048], P(None, 'mp', 'seq'), may hold values from -0.15625 to 0.15625
- value_weight: bfloat16 [1280, 2, 2048], P(None, 'mp', 'seq'), may hold values from -0.15625 to 0.15625
- gate: float32 [32], P('mp'), may hold values from 0.2 to 2
- cotangent: bfloat16 [16, 2048, 4096], P('dp', 'seq', 'mp'), may hold values from -6 to 6
Outputs:
- attended: bfloat16 [16, 2048, 4096], P('dp', 'seq', 'mp')
- query_grad: bfloat16 [16, 2048, 4096], P('dp', 'seq', 'mp')
- key_grad: float32 [1280, 2, 2048], P('dp', 'mp', 'seq')
- value_grad: float32 [1280, 2, 2048], P('dp', 'mp', 'seq')
Inputs may be any that keep to these rules, and one draw needn't show every extreme that they name: `image_slot`: within a document the images sit in distinct slots; each vision device (slots k * 3 to (k + 1) * 3 - 1) holds at most 3 of them, and some device holds exactly 3. `block_image`: within a document it never falls from one text block to the next, starts at 0, and names every one of the 16 images.
All inputs are finite; a program needn't handle non-finite values.
Results may differ from a plain program's by a relative error of at most 0.02.
The roundings to bfloat16 on the way count: a program that leaves them out, or rounds other values in their place, can miss the bound.
Values may be sent and summed in bfloat16 or wider, within the bound.
No kernel may reach another device: no remote copies, remote signals or barrier semaphores. Data moves between devices by JAX's collectives and lax.ppermute only.
A program may use at most 128 MiB of HBM per device.

v0:
```python
import math

import jax
import jax.numpy as jnp
from jax import lax
from jax.sharding import PartitionSpec as P


def body(query, latents, image_slot, block_image, key_weight, value_weight, gate, cotangent):
    seq_count = lax.axis_size("seq")
    tokens = query.shape[1]
    half_width = query.shape[2]
    head_count = gate.shape[0]
    head_size = half_width // head_count
    latent_count = latents.shape[2]
    latent_width = latents.shape[3]
    images = image_slot.shape[1]
    blocks_all = block_image.shape[1]
    block_size = tokens * seq_count // blocks_all
    blocks_here = tokens // block_size
    head_block = key_weight.shape[2]
    slot_of = image_slot[0]
    blocks_of = block_image[0]
    every_slot = lax.all_gather(latents[0], ("seq", "mp"), axis=0, tiled=True)
    chosen = jnp.take(every_slot, slot_of, axis=0)
    flat = chosen.reshape(images * latent_count, latent_width)
    keys = jnp.dot(flat, key_weight[:, 0, :], preferred_element_type=jnp.float32).astype(
        jnp.bfloat16
    )
    values = jnp.dot(flat, value_weight[:, 0, :], preferred_element_type=jnp.float32).astype(
        jnp.bfloat16
    )
    keys = keys.reshape(images, latent_count, head_block)
    values = values.reshape(images, latent_count, head_block)
    keys_all, values_all = (
        lax.all_gather(keys, "seq", axis=2, tiled=True),
        lax.all_gather(values, "seq", axis=2, tiled=True),
    )
    my_blocks = lax.dynamic_slice_in_dim(
        blocks_of, lax.axis_index("seq") * blocks_here, blocks_here
    )
    key_blocks = jnp.take(keys_all, my_blocks, axis=0)
    value_blocks = jnp.take(values_all, my_blocks, axis=0)
    scale = 1.0 / math.sqrt(head_size)
    gain = jnp.tanh(gate)[None, None, :, None]
    queries = query[0].reshape(blocks_here, block_size, head_count, head_size)
    key_heads = key_blocks.reshape(blocks_here, latent_count, head_count, head_size)
    value_heads = value_blocks.reshape(blocks_here, latent_count, head_count, head_size)
    score = (
        jnp.einsum("bthd,blhd->bhtl", queries, key_heads, preferred_element_type=jnp.float32)
        * scale
    )
    peak = jnp.max(score, axis=-1, keepdims=True)
    weights = jnp.exp(score - peak)
    prob = weights / jnp.sum(weights, axis=-1, keepdims=True)
    prob_low = prob.astype(jnp.bfloat16)
    mixed = jnp.einsum("bhtl,blhd->bthd", prob_low, value_heads, preferred_element_type=jnp.float32)
    attended = (mixed * gain).astype(jnp.bfloat16).reshape(1, tokens, half_width)
    gated = (
        cotangent[0].reshape(blocks_here, block_size, head_count, head_size).astype(jnp.float32)
        * gain
    ).astype(jnp.bfloat16)
    prob_grad = jnp.einsum(
        "bthd,blhd->bhtl", gated, value_heads, preferred_element_type=jnp.float32
    )
    delta = jnp.sum(prob_grad * prob, axis=-1, keepdims=True)
    score_grad = (prob * (prob_grad - delta) * scale).astype(jnp.bfloat16)
    query_grad = jnp.einsum(
        "bhtl,blhd->bthd", score_grad, key_heads, preferred_element_type=jnp.float32
    )
    query_grad = query_grad.astype(jnp.bfloat16).reshape(1, tokens, half_width)
    key_term = jnp.einsum(
        "bhtl,bthd->blhd", score_grad, queries, preferred_element_type=jnp.float32
    ).astype(jnp.bfloat16)
    value_term = jnp.einsum(
        "bhtl,bthd->blhd", prob_low, gated, preferred_element_type=jnp.float32
    ).astype(jnp.bfloat16)
    key_term = key_term.reshape(blocks_here, latent_count, half_width)
    value_term = value_term.reshape(blocks_here, latent_count, half_width)
    key_back, value_back = (
        lax.all_to_all(key_term, "seq", split_axis=2, concat_axis=0, tiled=True),
        lax.all_to_all(value_term, "seq", split_axis=2, concat_axis=0, tiled=True),
    )
    onehot = (blocks_of[None, :] == jnp.arange(images, dtype=jnp.int32)[:, None]).astype(
        jnp.bfloat16
    )
    key_image = jnp.einsum(
        "ib,blc->ilc", onehot, key_back, preferred_element_type=jnp.float32
    ).astype(jnp.bfloat16)
    value_image = jnp.einsum(
        "ib,blc->ilc", onehot, value_back, preferred_element_type=jnp.float32
    ).astype(jnp.bfloat16)
    grads_both = jnp.concatenate([key_image, value_image], axis=2).reshape(
        images * latent_count, 2 * head_block
    )
    row_count = latent_width // lax.axis_size("dp")
    summed = lax.psum_scatter(
        lax.dot_general(
            flat, grads_both, (((0,), (0,)), ((), ())), preferred_element_type=jnp.float32
        ).astype(jnp.bfloat16),
        "dp",
        scatter_dimension=0,
        tiled=True,
    ).astype(jnp.float32)
    key_grad = summed[:, :head_block].reshape(row_count, 1, head_block)
    value_grad = summed[:, head_block:].reshape(row_count, 1, head_block)
    return (attended, query_grad, key_grad, value_grad)


def solution(mesh):
    in_specs = (
        P("dp", "seq", "mp"),
        P("dp", ("seq", "mp"), None, None),
        P("dp", None),
        P("dp", None),
        P(None, "mp", "seq"),
        P(None, "mp", "seq"),
        P("mp"),
        P("dp", "seq", "mp"),
    )
    out_specs = (
        P("dp", "seq", "mp"),
        P("dp", "seq", "mp"),
        P("dp", "mp", "seq"),
        P("dp", "mp", "seq"),
    )
    return jax.shard_map(body, mesh=mesh, in_specs=in_specs, out_specs=out_specs, check_vma=False)
```

profile of v0, /device:TPU:38, one launch (start us, length us, event | category | flops | bytes accessed | tf_op | source)
XLA Modules:
  0.0 513.2 jit_solution(10913758557687621489)
XLA Ops:
  7.2 0.7 all-gather.9.cloned.1.call-update
  8.0 0.7 fusion.66
  8.6 0.7 compare_and_fusion.1
  9.3 60.3 %all-gather.9.cloned.1.call-done = bf16[1,48,64,1280]{3,2,0,1:T(8,128)(2,1)} async-done(((bf16[1,3,64,1280]{3,2,0,1:T(8,128)(2,1)}), bf16[1,48,64,1280]{3,2,0,1:T(8,128)(2,1)}) %all-gather.9.cloned.1.call-update) | async-done | bytes 7864336 | tf_op jit(solution)/shard_map/all_gather | solution.py:24
  69.6 3.9 gather_fusion
  73.5 0.3 broadcast_select_fusion
  73.9 1.7 convolution_convert_fusion
  75.7 3.5 convolution_convert_fusion.1
  79.2 1.2 copy.84
  80.6 0.4 copy.85
  81.0 0.3 copy-done.13
  81.4 33.8 %all-gather.7.cloned.1.call-done = bf16[16,64,2048]{2,1,0:T(8,128)(2,1)} async-done(((bf16[16,64,256]{2,1,0:T(8,128)(2,1)}), bf16[16,64,2048]{2,1,0:T(8,128)(2,1)}) %all-gather.7.cloned.1.call-update) | async-done | bytes 4194320 | tf_op jit(solution)/shard_map/all_gather | solution.py:36
  115.2 4.3 gather_fusion.2
  119.5 37.2 %all-gather.5.cloned.1.call-done = bf16[16,64,2048]{2,1,0:T(8,128)(2,1)} async-done(((bf16[16,64,256]{2,1,0:T(8,128)(2,1)}), bf16[16,64,2048]{2,1,0:T(8,128)(2,1)}) %all-gather.5.cloned.1.call-update) | async-done | bytes 4194320 | tf_op jit(solution)/shard_map/all_gather | solution.py:37
  156.6 4.2 gather_fusion.1
  160.9 4.1 select_bitcast_fusion
  165.0 1.2 fusion.9
  166.4 21.7 %fusion.74 = (f32[8,16,32]{2,1,0:T(8,128)S(1)}, f32[8,16,32,64]{3,2,1,0:T(8,128)S(1)}) fusion(f32[8,16,64,32]{2,3,1,0:T(8,128)S(1)} %fusion.9), kind=kOutput, calls=%fused_computation.78 | output fusion | flops 1048639 | bytes 2113536 | tf_op jit(solution)/shard_map/sub | solution.py:54
  188.1 1.4 copy-done.10
  189.5 3.2 convert_bitcast_fusion.1
  192.7 5.0 copy.77
  197.7 7.6 %reshape.186 = bf16[8,2,65536]{2,1,0:T(2,128)(2,1)} reshape(bf16[2048,8,64]{2,1,0:T(8,128)(2,1)} %bitcast.106) | data formatting | bytes 4194304
  205.3 5.4 %all-to-all-start.1 = ((bf16[8,2,65536]{2,1,0:T(2,128)(2,1)}), bf16[8,2,65536]{2,1,0:T(2,128)(2,1)}, u32[]{:S(2)}, u32[]{:S(2)}) async-start(bf16[8,2,65536]{2,1,0:T(2,128)(2,1)} %reshape.186), calls=%async_computation.1 | async-start | bytes 4194304 | tf_op jit(solution)/shard_map/all_to_all | solution.py:82
  210.7 4.2 fusion.3
  214.9 27.3 %convert_bitcast_fusion.2 = bf16[8,64,16,128]{3,1,2,0:T(8,128)(2,1)S(1)} fusion(f32[8,16,32,64]{3,2,1,0:T(8,128)} %fusion.3, bf16[8,32,16,128]{3,2,1,0:T(8,128)(2,1)} %bitcast.114, f32[8,16,32,64]{3,2,1,0:T(8,128)} %copy-done.10, f32[8,16,32]{2,1,0:T(8,128)S(1)} %get-tuple-element.27), kind=kOutput, calls=%fused_computation.30 | convolution fusion | flops 69996608 | bytes 5259264 | tf_op jit(solution)/shard_map/bhtl,bthd->blhd/dot_general | solution.py:72
  242.2 3.5 copy.74
  245.8 7.6 %reshape.188 = bf16[8,2,65536]{2,1,0:T(2,128)(2,1)} reshape(bf16[2048,8,64]{2,1,0:T(8,128)(2,1)} %bitcast.107) | data formatting | bytes 4194304
  253.3 4.8 all-to-all-start
  258.1 7.4 %reshape.187 = bf16[2048,8,64]{2,1,0:T(8,128)(2,1)} reshape(bf16[8,2,65536]{2,1,0:T(2,128)(2,1)} %all-to-all-done.1) | data formatting | bytes 4194304
  265.5 5.1 copy.69
  270.6 12.6 %all-to-all-done = bf16[8,2,65536]{2,1,0:T(2,128)(2,1)S(1)} async-done(((bf16[8,2,65536]{2,1,0:T(2,128)(2,1)}), bf16[8,2,65536]{2,1,0:T(2,128)(2,1)S(1)}, u32[]{:S(2)}, u32[]{:S(2)}) %all-to-all-start) | async-done | bytes 2097184 | tf_op jit(solution)/shard_map/all_to_all | solution.py:81
  283.3 5.0 reshape.189
  288.3 5.2 %copy.64 = bf16[8,8,64,256]{3,2,1,0:T(8,128)(2,1)} copy(bf16[8,8,64,256]{2,1,3,0:T(8,128)(2,1)} %bitcast.109) | data formatting | bytes 4194304 | tf_op jit(solution)/shard_map/all_to_all | solution.py:81
  293.5 1.2 fusion.48
  294.7 0.4 copy-done.3
  295.1 1.2 fusion.45
  296.4 0.4 copy-done.9
  296.8 3.1 fusion.2
  299.9 2.4 fusion.42
  302.3 1.4 copy.55
  303.7 2.3 reshape.146
  306.0 26.4 %fusion.37 = bf16[8,32,16,128]{3,1,2,0:T(8,128)(2,1)} fusion(bf16[8,8,16,8,128]{4,3,2,1,0:T(8,128)(2,1)S(1)} %copy-done.6, f32[8,16,32,64]{3,2,1,0:T(8,128)} %fusion.3, f32[8,16,32,64]{3,2,1,0:T(8,128)} %copy-done.10, f32[8,16,32]{2,1,0:T(8,128)S(1)} %get-tuple-element.27), kind=kOutput, calls=%fused_computation.41 | convolution fusion | flops 69472320 | bytes 5259264 | tf_op jit(solution)/shard_map/bhtl,blhd->bthd/dot_general | solution.py:68
  332.4 1.6 copy.59
  334.1 1.3 reshape.147
  335.3 168.9 %reduce-scatter.2.cloned.1.call-done = bf16[80,512]{1,0:T(8,128)(2,1)} async-done(((bf16[1280,512]{1,0:T(8,128)(2,1)}), bf16[80,512]{1,0:T(8,128)(2,1)}) %reduce-scatter.2.cloned.1.call-update) | async-done | bytes 81936 | tf_op jit(solution)/shard_map/reduce_scatter | solution.py:97
  504.3 0.9 convert_element_type.76
  505.2 0.7 copy.73
  505.9 0.7 copy.72
  (43 shorter events, 0.9 us)
Async XLA Ops:
  7.2 66.7 %copy-start = (bf16[1280,1,256]{2,0,1:T(8,128)(2,1)S(1)}, bf16[1280,1,256]{2,0,1:T(8,128)(2,1)}, u32[]{:S(2)}) copy-start(bf16[1280,1,256]{2,0,1:T(8,128)(2,1)} %param.14) | copy-start | bytes 1966084
  7.2 62.4 %all-gather.9.cloned.1.call-start = ((), (), s32[]{:S(2)}) async-start(), calls=%async_computation.6 | async-start | bytes 8355840 | tf_op jit(solution)/shard_map/all_gather | solution.py:24
  7.9 107.3 %all-gather.7.cloned.1.call-start = ((), (), s32[]{:S(2)}) async-start(), calls=%async_computation.4 | async-start | bytes 4718592 | tf_op jit(solution)/shard_map/all_gather | solution.py:36
  73.8 1.7 copy-start.8
  73.9 1.8 copy-start.14
  75.6 3.6 copy-start.15
  75.6 3.6 copy-start.12
  75.6 81.1 %all-gather.5.cloned.1.call-start = ((), (), s32[]{:S(2)}) async-start(), calls=%async_computation.3 | async-start | bytes 4718592 | tf_op jit(solution)/shard_map/all_gather | solution.py:37
  79.1 1.3 copy-start.11
  80.6 0.7 copy-start.13
  160.9 4.1 copy-start.7
  165.0 1.4 copy-start.5
  188.1 1.4 copy-start.10
  205.3 48.1 %all-to-all-start.1 = ((bf16[8,2,65536]{2,1,0:T(2,128)(2,1)}), bf16[8,2,65536]{2,1,0:T(2,128)(2,1)}, u32[]{:S(2)}, u32[]{:S(2)}) async-start(bf16[8,2,65536]{2,1,0:T(2,128)(2,1)} %reshape.186), calls=%async_computation.1 | async-start | bytes 4194304 | tf_op jit(solution)/shard_map/all_to_all | solution.py:82
  253.3 29.9 %all-to-all-start = ((bf16[8,2,65536]{2,1,0:T(2,128)(2,1)}), bf16[8,2,65536]{2,1,0:T(2,128)(2,1)S(1)}, u32[]{:S(2)}, u32[]{:S(2)}) async-start(bf16[8,2,65536]{2,1,0:T(2,128)(2,1)} %reshape.188), calls=%async_computation | async-start | bytes 4194304 | tf_op jit(solution)/shard_map/all_to_all | solution.py:81
  258.1 246.1 %reduce-scatter.2.cloned.1.call-start = ((), (), s32[]{:S(2)}) async-start(), calls=%async_computation.5 | async-start | bytes 1392640 | tf_op jit(solution)/shard_map/reduce_scatter | solution.py:97
  288.2 5.2 %copy-start.2 = (bf16[8,8,64,256]{3,2,1,0:T(8,128)(2,1)S(1)}, bf16[8,8,64,256]{3,2,1,0:T(8,128)(2,1)}, u32[]{:S(2)}) copy-start(bf16[8,8,64,256]{3,2,1,0:T(8,128)(2,1)} %copy.69) | copy-start | bytes 6291460
  293.5 1.6 copy-start.3
  295.1 1.7 copy-start.9
  296.8 3.1 copy-start.4
  302.3 3.7 copy-start.6
  306.0 200.7 %copy-start.1 = (bf16[1280,1,256]{2,0,1:T(8,128)(2,1)S(1)}, bf16[1280,1,256]{2,0,1:T(8,128)(2,1)}, u32[]{:S(2)}) copy-start(bf16[1280,1,256]{2,0,1:T(8,128)(2,1)} %param.14) | copy-start | bytes 1966084
Sparse Core Ops, SparseCore 0:
  9.8 59.7 all-gather.8
  75.7 39.4 all-gather.6
  117.0 39.5 all-gather.4
  300.0 204.1 reduce-scatter.1
where the time goes:
time: 516 us; the launch traced here: 513 us
  waiting for transfers between devices  314 us (61%)
  matrix products  75.4 us (15%)
  local copies, waits for them, and re-layouts  71.1 us (14%)
  other arithmetic  28.8 us (6%)
  between operations  14 us (3%)
  starting transfers between devices  10.4 us (2%)
    reduce_scatter x1, waiting for transfers between devices, body(): lax.psum_scatter(lax.dot_general(flat, grads_both, (((0,), (0,)), ((), ()...  169 us
    all_gather x1, waiting for transfers between devices, body(): every_slot = lax.all_gather(latents[0], ('seq', 'mp'), axis=0, tiled=True)  60.3 us
    all_gather x1, waiting for transfers between devices, body(): lax.all_gather(values, 'seq', axis=2, tiled=True)  37.2 us
    all_gather x1, waiting for transfers between devices, body(): lax.all_gather(keys, 'seq', axis=2, tiled=True)  33.8 us
    unnamed x40, local copies, waits for them, and re-layouts  33.2 us
    dot_general x1, matrix products, body(): jnp.einsum('bhtl,bthd->blhd', score_grad, queries, preferred_element_type...  27.3 us
    dot_general x1, matrix products, body(): jnp.einsum('bhtl,blhd->bthd', score_grad, key_heads, preferred_element_ty...  26.4 us
    sub x1, other arithmetic, body(): weights = jnp.exp(score - peak)  21.7 us
  transfers between devices with their start and end apart: 6, of which 5 were waited for; matrix products, arithmetic and copies ran while one was open for 20% of the time, Pallas kernels for 0%

commit v1 on v0

v1 whole, which is shorter than its diff:
```python
import math

import jax
import jax.numpy as jnp
from jax import lax
from jax.experimental import pallas as pl
from jax.experimental.pallas import tpu as pltpu
from jax.sharding import PartitionSpec as P

F32, BF16 = jnp.float32, jnp.bfloat16
IMAGES, LAT, HD, TB, UNROLL = 16, 64, 128, 32, 8
PIECES = 8
ROWS = LAT // PIECES
VMEM = pl.BlockSpec(memory_space=pltpu.VMEM)
SMEM = pl.BlockSpec(memory_space=pltpu.SMEM)


def dot(a, b):
    return jnp.dot(a, b, preferred_element_type=F32)


def dot_t(a, b):
    return lax.dot_general(a, b, (((0,), (0,)), ((), ())), preferred_element_type=F32)


def project_kernel(own, left, right, far, sib, wk, wv, kz, vz, kzt, vzt, kf, vf):
    span = IMAGES * ROWS
    parts = [own, left, right, far] + [sib.at[j] for j in range(4)]
    for p, part in enumerate(parts):
        rows = part[...]
        kf[p * span : (p + 1) * span, :] = dot(rows, wk[...])
        vf[p * span : (p + 1) * span, :] = dot(rows, wv[...])
    zero = jnp.zeros((LAT, HD), F32)
    for i in range(IMAGES):
        for src, plain, turned in ((kf, kz, kzt), (vf, vz, vzt)):
            x = jnp.concatenate(
                [src[p * span + i * ROWS : p * span + (i + 1) * ROWS, :] for p in range(PIECES)], axis=0
            )
            top = jnp.concatenate([x[:, :HD], zero], axis=1)
            low = jnp.concatenate([zero, x[:, HD:]], axis=1)
            both = jnp.concatenate([top, low], axis=0)
            plain[i] = both.astype(BF16)
            turned[i] = both.T.astype(BF16)


def attend_kernel(blk, gain, q, c, kz, vz, kzt, vzt, att, qg, ki, acck, accv):
    scale = 1.0 / math.sqrt(HD)
    c2 = scale * math.log2(math.e)
    acck[...] = jnp.zeros_like(acck)
    accv[...] = jnp.zeros_like(accv)
    g = gain[...]

    def body(step, carry):
        base = step * UNROLL
        first = lax.broadcasted_iota(jnp.int32, (TB * UNROLL, 2 * LAT), 1) < LAT

        def halves(x, op, fill):
            a = op(jnp.where(first, x, fill), axis=1, keepdims=True)
            b = op(jnp.where(first, fill, x), axis=1, keepdims=True)
            return jnp.where(first, a, b)

        at = [pl.ds(pl.multiple_of((base + u) * TB, TB), TB) for u in range(UNROLL)]
        img = [blk[base + u] for u in range(UNROLL)]
        qs = [q[a, :] for a in at]
        gs = [(c[a, :].astype(F32) * g).astype(BF16) for a in at]
        s = jnp.concatenate([dot(qs[u], kzt[img[u]]) for u in range(UNROLL)], axis=0)
        pg = jnp.concatenate([dot(gs[u], vzt[img[u]]) for u in range(UNROLL)], axis=0)
        peak = halves(s, jnp.max, -jnp.inf)
        e = jnp.exp2((s - peak) * c2)
        prob = e / halves(e, jnp.sum, 0.0)
        low = prob.astype(BF16)
        delta = halves(prob * pg, jnp.sum, 0.0)
        sg = (prob * (pg - delta) * scale).astype(BF16)
        for u in range(UNROLL):
            lu, su = low[u * TB : (u + 1) * TB, :], sg[u * TB : (u + 1) * TB, :]
            att[at[u], :] = (dot(lu, vz[img[u]]) * g).astype(BF16)
            qg[at[u], :] = dot(su, kz[img[u]]).astype(BF16)
            kt = dot_t(su, qs[u])
            vt = dot_t(lu, gs[u])
            rows = pl.ds(pl.multiple_of(img[u] * LAT, LAT), LAT)
            acck[rows, :HD] += kt[:LAT, :HD]
            acck[rows, HD:] += kt[LAT:, HD:]
            accv[rows, :HD] += vt[:LAT, :HD]
            accv[rows, HD:] += vt[LAT:, HD:]
        return carry

    lax.fori_loop(0, blk.shape[0] // UNROLL, body, 0)
    span = IMAGES * ROWS
    for p in range(PIECES):
        for acc, lo in ((acck, 0), (accv, 2 * HD)):
            x = jnp.concatenate(
                [acc[i * LAT + p * ROWS : i * LAT + (p + 1) * ROWS, :] for i in range(IMAGES)], axis=0
            )
            ki[p * span : (p + 1) * span, lo : lo + 2 * HD] = x.astype(BF16)


def swap(x, axes, pairs):
    return lax.ppermute(x, axes, pairs)


def exchange(x, axes, **kw):
    return lax.all_to_all(x, axes, split_axis=0, concat_axis=0, tiled=True, **kw)


def body(query, latents, image_slot, block_image, key_weight, value_weight, gate, cotangent):
    seq_i, mp_i, dp_i = lax.axis_index("seq"), lax.axis_index("mp"), lax.axis_index("dp")
    tokens, width = query.shape[1], query.shape[2]
    kv = latents.shape[3]
    n_seq = 8
    cols = width // n_seq
    slots = latents.shape[1]
    half = kv // 2
    cut = latents[0].reshape(slots, PIECES, ROWS, 2, half).transpose(1, 3, 0, 2, 4)
    got = exchange(cut.reshape(16, slots * ROWS, half), ("seq", "mp"))
    mine = jnp.take(got.reshape(16 * slots, ROWS, half), image_slot[0], axis=0)
    mine = mine.reshape(IMAGES * ROWS, half)
    other = swap(mine, "mp", [(0, 1), (1, 0)])
    own = jnp.where(
        mp_i == 0, jnp.concatenate([mine, other], axis=1), jnp.concatenate([other, mine], axis=1)
    )

    def along_x(d):
        return [(x * 2 + k, ((x + d) % 4) * 2 + k) for x in range(4) for k in range(2)]

    left = swap(own, "seq", along_x(1))
    right = swap(own, "seq", along_x(-1))
    far = swap(own, "seq", along_x(2))
    here = jnp.stack([own, left, right, far])
    sib = swap(here, "seq", [(j, j ^ 1) for j in range(8)])
    wk, wv = key_weight[:, 0, :], value_weight[:, 0, :]
    shape = jax.ShapeDtypeStruct
    zs, zt = shape((IMAGES, 2 * LAT, 2 * HD), BF16), shape((IMAGES, 2 * HD, 2 * LAT), BF16)
    n_rows = IMAGES * LAT
    kz, vz, kzt, vzt = pl.pallas_call(
        project_kernel,
        out_shape=(zs, zs, zt, zt),
        in_specs=[VMEM] * 7,
        out_specs=(VMEM,) * 4,
        scratch_shapes=[pltpu.VMEM((n_rows, 2 * HD), F32)] * 2,
        compiler_params=pltpu.CompilerParams(vmem_limit_bytes=24 * 2**20),
        cost_estimate=pl.CostEstimate(
            flops=2 * n_rows * kv * 512, bytes_accessed=8 * 2**20, transcendentals=0
        ),
        name="project",
    )(own, left, right, far, sib, wk, wv)

    def to_heads(x):
        y = exchange(x[0].reshape(tokens, n_seq, cols).transpose(1, 0, 2), "seq")
        return y.reshape(n_seq * tokens, cols)

    q_all, c_all = to_heads(query), to_heads(cotangent)
    gain = jnp.repeat(jnp.tanh(lax.dynamic_slice_in_dim(gate, seq_i * 2, 2)), HD)[None, :]
    full = shape((n_seq * tokens, cols), BF16)
    att, qg, ki = pl.pallas_call(
        attend_kernel,
        out_shape=(full, full, shape((n_rows, 4 * HD), BF16)),
        in_specs=[SMEM] + [VMEM] * 7,
        out_specs=(VMEM,) * 3,
        scratch_shapes=[pltpu.VMEM((n_rows, 2 * HD), F32)] * 2,
        compiler_params=pltpu.CompilerParams(vmem_limit_bytes=24 * 2**20),
        cost_estimate=pl.CostEstimate(
            flops=2**32, bytes_accessed=11 * 2**20, transcendentals=2**19
        ),
        name="attend",
    )(block_image[0], gain, q_all, c_all, kz, vz, kzt, vzt)

    def to_tokens(x):
        y = exchange(x.reshape(n_seq, tokens, cols), "seq")
        return y.transpose(1, 0, 2).reshape(1, tokens, width)

    attended, query_grad = to_tokens(att), to_tokens(qg)

    flat = jnp.concatenate([here, sib], axis=0).reshape(n_rows, kv)
    part = dot_t(flat, ki).astype(BF16)
    rows = kv // 16
    part = part.reshape(4, 2, 2, rows, 4 * HD)
    z_i, h_i = dp_i // 2, dp_i % 2
    z_odd = z_i % 2
    pairs = []
    for z in range(8):
        for h in range(2):
            for s in range(8):
                if s % 2 == 0:
                    to = z ^ 1
                else:
                    to = (z + 1) % 8 if z % 2 else (z - 1) % 8
                pairs.append(((z * 2 + h) * 8 + s, (to * 2 + h) * 8 + s))

    def pick(x, i, axis):
        return lax.dynamic_index_in_dim(x, i, axis, keepdims=False)

    def join(x, y):
        return (x.astype(F32) + y.astype(F32)).astype(BF16)

    part = join(pick(part, z_odd, 1), swap(pick(part, 1 - z_odd, 1), ("dp", "seq"), pairs))
    part = join(pick(part, h_i, 1), swap(pick(part, 1 - h_i, 1), "dp", [(j, j ^ 1) for j in range(16)]))
    groups = [[(k * 2 + odd) * 2 + h for k in range(4)] for odd in range(2) for h in range(2)]
    total = exchange(part, "dp", axis_index_groups=groups).astype(F32).sum(axis=0)
    key_grad = total[:, : 2 * HD].reshape(rows, 1, 2 * HD)
    value_grad = total[:, 2 * HD :].reshape(rows, 1, 2 * HD)
    return attended, query_grad, key_grad, value_grad


def solution(mesh):
    in_specs = (
        P("dp", "seq", "mp"),
        P("dp", ("seq", "mp"), None, None),
        P("dp", None),
        P("dp", None),
        P(None, "mp", "seq"),
        P(None, "mp", "seq"),
        P("mp"),
        P("dp", "seq", "mp"),
    )
    out_specs = (
        P("dp", "seq", "mp"),
        P("dp", "seq", "mp"),
        P("dp", "mp", "seq"),
        P("dp", "mp", "seq"),
    )
    return jax.shard_map(body, mesh=mesh, in_specs=in_specs, out_specs=out_specs, check_vma=False)
```

time: 516 us -> 156 us (0.30)
  waiting for transfers between devices: 314 us -> 56.7 us
  matrix products: 75.4 us -> 3.29 us
  local copies, waits for them, and re-layouts: 71.1 us -> 28.5 us
  starting transfers between devices: 10.4 us -> 46.1 us
  other arithmetic: 28.8 us -> 4.47 us
  Pallas kernels: 0 us -> 13.6 us
  between operations: 14 us -> 0.82 us
    reduce_scatter x1 -> x0, waiting for transfers between devices: 169 us -> none  [body(): lax.psum_scatter(lax.dot_general(flat, grads_both, (((0,), (0,)), ((), ()...]
    all_gather x3 -> x0, waiting for transfers between devices: 131 us -> none  [the longest x1 60.3 us: body(): every_slot = lax.all_gather(latents[0], ('seq', 'mp'), axis=0, tiled=True)]
    dot_general x11 -> x1, matrix products: 75.4 us -> 3.29 us  [dot_t(): lax.dot_general(a, b, (((0,), (0,)), ((), ())), preferred_element_type=F32)]
    ppermute x0 -> x7, waiting for transfers between devices: none -> 28.4 us  [swap(): return lax.ppermute(x, axes, pairs)]
    all_to_all x2 -> x6, starting transfers between devices: 10.2 us -> 37.4 us  [exchange(): lax.all_to_all(x, axes, split_axis=0, concat_axis=0, tiled=True, **kw)]
    sub x1 -> x0, other arithmetic: 21.7 us -> none  [body(): weights = jnp.exp(score - peak)]
    unnamed x40 -> x45, local copies, waits for them, and re-layouts: 33.2 us -> 15.8 us
    all_to_all x2 -> x6, waiting for transfers between devices: 12.6 us -> 28.3 us  [exchange(): lax.all_to_all(x, axes, split_axis=0, concat_axis=0, tiled=True, **kw)]
  transfers between devices with their start and end apart: 6 -> 13, of which waited for: 5 -> 9; matrix products, arithmetic and copies ran while one was open for 20% -> 12% of each run, Pallas kernels for 0% -> 1%
where the time goes in v1:
time: 156 us; the launch traced here: 154 us
  waiting for transfers between devices  56.7 us (36%)
  starting transfers between devices  46.1 us (30%)
  local copies, waits for them, and re-layouts  28.5 us (18%)
  Pallas kernels  13.6 us (9%)
  other arithmetic  4.47 us (3%)
  matrix products  3.29 us (2%)
    all_to_all x6, starting transfers between devices, exchange(): lax.all_to_all(x, axes, split_axis=0, concat_axis=0, tiled=True, **kw)  37.4 us
    ppermute x7, waiting for transfers between devices, swap(): return lax.ppermute(x, axes, pairs)  28.4 us
    all_to_all x6, waiting for transfers between devices, exchange(): lax.all_to_all(x, axes, split_axis=0, concat_axis=0, tiled=True, **kw)  28.3 us
    unnamed x45, local copies, waits for them, and re-layouts  15.8 us
    pallas_call x1, Pallas kernels, body(): pl.pallas_call(attend_kernel, out_shape=(full, full, shape((n_rows, 4 * H...  11.4 us
    ppermute x7, starting transfers between devices, swap(): return lax.ppermute(x, axes, pairs)  8.71 us
    dot_general x1, matrix products, dot_t(): lax.dot_general(a, b, (((0,), (0,)), ((), ())), preferred_element_type=F32)  3.29 us
  transfers between devices with their start and end apart: 13, of which 9 were waited for; matrix products, arithmetic and copies ran while one was open for 12% of the time, Pallas kernels for 1%

profile of v1, /device:TPU:38, one launch (start us, length us, event | category | flops | bytes accessed | tf_op | source)
XLA Modules:
  0.0 153.5 jit_solution(3948451417498150673)
XLA Ops:
  0.7 1.2 reshape_squeeze.11
  1.9 0.8 copy.22
  2.7 5.8 %all-to-all-start.2 = ((bf16[16,24,640]{2,1,0:T(8,128)(2,1)}), bf16[16,24,640]{2,1,0:T(8,128)(2,1)S(1)}, u32[]{:S(2)}, u32[]{:S(2)}) async-start(bf16[16,24,640]{2,1,0:T(8,128)(2,1)} %bitcast.8), calls=%async_computation.2 | async-start | bytes 983040 | tf_op jit(solution)/shard_map/all_to_all | solution.py:102
  8.7 7.7 %all-to-all-done.2 = bf16[16,24,640]{2,1,0:T(8,128)(2,1)S(1)} async-done(((bf16[16,24,640]{2,1,0:T(8,128)(2,1)}), bf16[16,24,640]{2,1,0:T(8,128)(2,1)S(1)}, u32[]{:S(2)}, u32[]{:S(2)}) %all-to-all-start.2) | async-done | bytes 491552 | tf_op jit(solution)/shard_map/all_to_all | solution.py:102
  17.2 0.9 collective-permute-start
  18.3 1.2 copy.30
  19.5 6.2 %all-to-all-start = ((bf16[8,256,256]{2,1,0:T(8,128)(2,1)}), bf16[8,256,256]{2,1,0:T(8,128)(2,1)S(1)}, u32[]{:S(2)}, u32[]{:S(2)}) async-start(bf16[8,256,256]{2,1,0:T(8,128)(2,1)} %bitcast.59), calls=%async_computation | async-start | bytes 2097152 | tf_op jit(solution)/shard_map/all_to_all | solution.py:102
  26.1 1.2 copy.29
  27.4 1.5 collective-permute-start.3
  29.0 3.2 %collective-permute-start.1 = (bf16[128,1280]{1,0:T(8,128)(2,1)S(1)}, bf16[128,1280]{1,0:T(8,128)(2,1)S(1)}, u32[]{:S(2)}, u32[]{:S(2)}) collective-permute-start(bf16[128,1280]{1,0:T(8,128)(2,1)S(1)} %maximum_select_fusion.own), channel_id=1, source_target_pairs={{0,4},{2,6},{4,8},{6,10},{8,12},{10,14},{12,0},{14,2},{1,5},{3,7},... | collective-permute-start | bytes 983048 | tf_op jit(solution)/shard_map/ppermute | solution.py:98
  32.3 0.8 constant_dynamic-update-slice_fusion.4
  33.1 14.1 %collective-permute-done.3.far = bf16[128,1280]{1,0:T(8,128)(2,1)S(1)} collective-permute-done((bf16[128,1280]{1,0:T(8,128)(2,1)S(1)}, bf16[128,1280]{1,0:T(8,128)(2,1)S(1)}, u32[]{:S(2)}, u32[]{:S(2)}) %collective-permute-start.3) | collective-permute-done | bytes 327712 | tf_op jit(solution)/shard_map/ppermute | solution.py:98
  47.2 5.4 %collective-permute-done.2.right = bf16[128,1280]{1,0:T(8,128)(2,1)S(1)} collective-permute-done((bf16[128,1280]{1,0:T(8,128)(2,1)S(1)}, bf16[128,1280]{1,0:T(8,128)(2,1)S(1)}, u32[]{:S(2)}, u32[]{:S(2)}) %collective-permute-start.2) | collective-permute-done | bytes 327712 | tf_op jit(solution)/shard_map/ppermute | solution.py:98
  53.1 1.3 pad_maximum_fusion
  54.4 0.8 constant_dynamic-update-slice_fusion.3
  55.1 6.5 %all-to-all-start.1 = ((bf16[8,256,256]{2,1,0:T(8,128)(2,1)}), bf16[8,256,256]{2,1,0:T(8,128)(2,1)}, u32[]{:S(2)}, u32[]{:S(2)}) async-start(bf16[8,256,256]{2,1,0:T(8,128)(2,1)} %bitcast.69), calls=%async_computation.1 | async-start | bytes 2097152 | tf_op jit(solution)/shard_map/all_to_all | solution.py:102
  61.6 0.8 constant_dynamic-update-slice_fusion.2
  62.4 0.7 constant_dynamic-update-slice_fusion.1
  63.2 1.0 copy-done.1
  64.1 1.1 copy-done.2
  65.2 1.1 copy-done.3
  66.3 2.2 %project.1 = (bf16[16,128,256]{2,1,0:T(8,128)(2,1)S(1)}, bf16[16,128,256]{2,1,0:T(8,128)(2,1)S(1)}, bf16[16,256,128]{2,1,0:T(8,128)(2,1)S(1)}, bf16[16,256,128]{2,1,0:T(8,128)(2,1)S(1)}) custom-call(bf16[128,1280]{1,0:T(8,128)(2,1)S(1)} %copy-done.1, bf16[128,1280]{1,0:T(8,128)(2,1)S(1)} %collective-permute-done.1.left, ...), custom_call_target="tpu_custom_call" | custom-call | flops 1342177280 | bytes 8388608 | tf_op jit(solution)/shard_map/project/pallas_call | solution.py:134
  68.5 1.0 copy-done.5
  69.5 1.0 copy-done.7
  70.5 1.0 copy-done.9
  71.5 1.0 copy-done.11
  72.5 3.2 %all-to-all-done.1 = bf16[8,256,256]{2,1,0:T(8,128)(2,1)} async-done(((bf16[8,256,256]{2,1,0:T(8,128)(2,1)}), bf16[8,256,256]{2,1,0:T(8,128)(2,1)}, u32[]{:S(2)}, u32[]{:S(2)}) %all-to-all-start.1) | async-done | bytes 1048608 | tf_op jit(solution)/shard_map/all_to_all | solution.py:102
  75.7 1.2 copy-done.6
  76.9 1.2 copy-done.8
  78.2 1.2 copy-done.10
  79.4 1.2 copy-done.12
  80.6 11.4 %attend.1 = (bf16[2048,256]{1,0:T(8,128)(2,1)}, bf16[2048,256]{1,0:T(8,128)(2,1)}, bf16[1024,512]{1,0:T(8,128)(2,1)S(1)}) custom-call(s32[64]{0:T(128)S(1)} %bitcast.66, f32[1,256]{1,0:T(1,128)S(1)} %bitcast.67, bf16[2048,256]{1,0:T(8,128)(2,1)S(1)} %bitcast.63, bf16[2048,256]{1,0:T(8,128)(2,1)} %bitcast.5.c, bf16[16,128,256]{2,1,0:T(8,128)(2,1)S(1)} %copy-done.6, ...), custom_call_target="tpu_custom_call" | custom-call | flops 4294967296 | bytes 11534336 | tf_op jit(solution)/shard_map/attend/pallas_call | solution.py:154
  92.0 1.0 copy-done.13
  93.0 5.7 %all-to-all-start.4 = ((bf16[8,256,256]{2,1,0:T(8,128)(2,1)}), bf16[8,256,256]{2,1,0:T(8,128)(2,1)S(1)}, u32[]{:S(2)}, u32[]{:S(2)}) async-start(bf16[8,256,256]{2,1,0:T(8,128)(2,1)} %bitcast.22), calls=%async_computation.4 | async-start | bytes 2097152 | tf_op jit(solution)/shard_map/all_to_all | solution.py:102
  98.7 1.2 constant_dynamic-update-slice_fusion
  99.9 3.3 %convolution_convert_fusion = bf16[1280,512]{1,0:T(8,128)(2,1)S(1)} fusion(bf16[1024,1280]{1,0:T(8,128)(2,1)} %bitcast.24, bf16[1024,512]{1,0:T(8,128)(2,1)S(1)} %copy-done.14), kind=kOutput, calls=%fused_computation.1 | convolution fusion | flops 1342832640 | bytes 4980736 | tf_op jit(solution)/shard_map/dot_general | solution.py:23
  103.2 1.0 dynamic-slice_bitcast_fusion
  104.3 8.3 %all-to-all-done.4 = bf16[8,256,256]{2,1,0:T(8,128)(2,1)S(1)} async-done(((bf16[8,256,256]{2,1,0:T(8,128)(2,1)}), bf16[8,256,256]{2,1,0:T(8,128)(2,1)S(1)}, u32[]{:S(2)}, u32[]{:S(2)}) %all-to-all-start.4) | async-done | bytes 1048608 | tf_op jit(solution)/shard_map/all_to_all | solution.py:102
  112.6 5.6 %all-to-all-start.3 = ((bf16[8,256,256]{2,1,0:T(8,128)(2,1)}), bf16[8,256,256]{2,1,0:T(8,128)(2,1)S(1)}, u32[]{:S(2)}, u32[]{:S(2)}) async-start(bf16[8,256,256]{2,1,0:T(8,128)(2,1)} %bitcast.20), calls=%async_computation.3 | async-start | bytes 2097152 | tf_op jit(solution)/shard_map/all_to_all | solution.py:102
  118.2 1.3 fusion
  119.5 3.0 %collective-permute-start.6 = (bf16[4,80,512]{2,1,0:T(8,128)(2,1)S(1)}, bf16[4,80,512]{2,1,0:T(8,128)(2,1)S(1)}, u32[]{:S(2)}, u32[]{:S(2)}) collective-permute-start(bf16[4,80,512]{2,1,0:T(8,128)(2,1)S(1)} %dynamic-slice_bitcast_fusion.1), channel_id=1, source_target_pairs={{0,16},{16,0},{32,48},{48,32},{64,80},{80,64},{96,112},{112,96},{1... | collective-permute-start | bytes 983048 | tf_op jit(solution)/shard_map/ppermute | solution.py:98
  122.5 8.4 %collective-permute-done.6 = bf16[4,80,512]{2,1,0:T(8,128)(2,1)S(1)} collective-permute-done((bf16[4,80,512]{2,1,0:T(8,128)(2,1)S(1)}, bf16[4,80,512]{2,1,0:T(8,128)(2,1)S(1)}, u32[]{:S(2)}, u32[]{:S(2)}) %collective-permute-start.6) | collective-permute-done | bytes 327712 | tf_op jit(solution)/shard_map/ppermute | solution.py:98
  130.9 0.8 fusion.1
  132.1 7.6 %all-to-all-start.5 = ((bf16[4,80,512]{2,1,0:T(8,128)(2,1)}), bf16[4,80,512]{2,1,0:T(8,128)(2,1)S(1)}, u32[]{:S(2)}, u32[]{:S(2)}) async-start(bf16[4,80,512]{2,1,0:T(8,128)(2,1)} %fusion.1), calls=%async_computation.5 | async-start | bytes 655360 | tf_op jit(solution)/shard_map/all_to_all | solution.py:102
  140.2 1.3 reshape.171
  142.1 1.3 reshape.169
  143.4 8.6 %all-to-all-done.5 = bf16[4,80,512]{2,1,0:T(8,128)(2,1)S(1)} async-done(((bf16[4,80,512]{2,1,0:T(8,128)(2,1)}), bf16[4,80,512]{2,1,0:T(8,128)(2,1)S(1)}, u32[]{:S(2)}, u32[]{:S(2)}) %all-to-all-start.5) | async-done | bytes 327712 | tf_op jit(solution)/shard_map/all_to_all | solution.py:102
  152.1 0.7 reshape.175
  (56 shorter events, 4.9 us)
Async XLA Ops:
  0.6 7.9 %copy-start.18 = (s32[1,16]{1,0:T(1,128)S(1)}, s32[1,16]{1,0:T(1,128)}, u32[]{:S(2)}) copy-start(s32[1,16]{1,0:T(1,128)} %param.10) | copy-start | bytes 196
  0.6 17.4 %copy-start.16 = (bf16[1,256,2048]{2,1,0:T(8,128)(2,1)S(1)}, bf16[1,256,2048]{2,1,0:T(8,128)(2,1)}, u32[]{:S(2)}) copy-start(bf16[1,256,2048]{2,1,0:T(8,128)(2,1)} %param.8) | copy-start | bytes 3145732
  2.7 13.8 %all-to-all-start.2 = ((bf16[16,24,640]{2,1,0:T(8,128)(2,1)}), bf16[16,24,640]{2,1,0:T(8,128)(2,1)S(1)}, u32[]{:S(2)}, u32[]{:S(2)}) async-start(bf16[16,24,640]{2,1,0:T(8,128)(2,1)} %bitcast.8), calls=%async_computation.2 | async-start | bytes 983040 | tf_op jit(solution)/shard_map/all_to_all | solution.py:102
  17.2 10.2 %collective-permute-start = (bf16[128,640]{1,0:T(8,128)(2,1)S(1)}, bf16[128,640]{1,0:T(8,128)(2,1)S(1)}, u32[]{:S(2)}, u32[]{:S(2)}) collective-permute-start(bf16[128,640]{1,0:T(8,128)(2,1)S(1)} %bitcast_select_fusion), channel_id=1, source_target_pairs={{0,1},{1,0},{2,3},{3,2},{4,5},{5,4},{6,7},{7,6},{8,9},{9,8},{10,11... | collective-permute-start | bytes 491528 | tf_op jit(solution)/shard_map/ppermute | solution.py:98
  18.3 7.4 %copy-start.17 = (bf16[1,256,2048]{2,1,0:T(8,128)(2,1)S(1)}, bf16[1,256,2048]{2,1,0:T(8,128)(2,1)}, u32[]{:S(2)}) copy-start(bf16[1,256,2048]{2,1,0:T(8,128)(2,1)} %param.15) | copy-start | bytes 3145732
  19.5 35.6 %all-to-all-start = ((bf16[8,256,256]{2,1,0:T(8,128)(2,1)}), bf16[8,256,256]{2,1,0:T(8,128)(2,1)S(1)}, u32[]{:S(2)}, u32[]{:S(2)}) async-start(bf16[8,256,256]{2,1,0:T(8,128)(2,1)} %bitcast.59), calls=%async_computation | async-start | bytes 2097152 | tf_op jit(solution)/shard_map/all_to_all | solution.py:102
  25.8 1.5 copy-start.19
  27.4 25.7 %copy-start = (bf16[128,1280]{1,0:T(8,128)(2,1)}, bf16[128,1280]{1,0:T(8,128)(2,1)S(1)}, u32[]{:S(2)}) copy-start(bf16[128,1280]{1,0:T(8,128)(2,1)S(1)} %maximum_select_fusion.own) | copy-start | bytes 983044
  27.4 19.7 %collective-permute-start.3 = (bf16[128,1280]{1,0:T(8,128)(2,1)S(1)}, bf16[128,1280]{1,0:T(8,128)(2,1)S(1)}, u32[]{:S(2)}, u32[]{:S(2)}) collective-permute-start(bf16[128,1280]{1,0:T(8,128)(2,1)S(1)} %maximum_select_fusion.own), channel_id=1, source_target_pairs={{0,8},{2,10},{4,12},{6,14},{8,0},{10,2},{12,4},{14,6},{1,9},{3,11}... | collective-permute-start | bytes 983048 | tf_op jit(solution)/shard_map/ppermute | solution.py:98
  29.0 23.6 %collective-permute-start.2 = (bf16[128,1280]{1,0:T(8,128)(2,1)S(1)}, bf16[128,1280]{1,0:T(8,128)(2,1)S(1)}, u32[]{:S(2)}, u32[]{:S(2)}) collective-permute-start(bf16[128,1280]{1,0:T(8,128)(2,1)S(1)} %maximum_select_fusion.own), channel_id=1, source_target_pairs={{0,12},{2,14},{4,0},{6,2},{8,4},{10,6},{12,8},{14,10},{1,13},{3,15... | collective-permute-start | bytes 983048 | tf_op jit(solution)/shard_map/ppermute | solution.py:98
  29.0 24.2 %collective-permute-start.1 = (bf16[128,1280]{1,0:T(8,128)(2,1)S(1)}, bf16[128,1280]{1,0:T(8,128)(2,1)S(1)}, u32[]{:S(2)}, u32[]{:S(2)}) collective-permute-start(bf16[128,1280]{1,0:T(8,128)(2,1)S(1)} %maximum_select_fusion.own), channel_id=1, source_target_pairs={{0,4},{2,6},{4,8},{6,10},{8,12},{10,14},{12,0},{14,2},{1,5},{3,7},... | collective-permute-start | bytes 983048 | tf_op jit(solution)/shard_map/ppermute | solution.py:98
  54.4 8.8 %collective-permute-start.4 = (bf16[4,128,1280]{2,1,0:T(8,128)(2,1)}, bf16[4,128,1280]{2,1,0:T(8,128)(2,1)S(1)}, u32[]{:S(2)}, u32[]{:S(2)}) collective-permute-start(bf16[4,128,1280]{2,1,0:T(8,128)(2,1)} %pad_maximum_fusion), channel_id=1, source_target_pairs={{0,2},{2,0},{4,6},{6,4},{8,10},{10,8},{12,14},{14,12},{1,3},{3,1},... | collective-permute-start | bytes 3932168 | tf_op jit(solution)/shard_map/ppermute | solution.py:98
  55.1 20.5 %all-to-all-start.1 = ((bf16[8,256,256]{2,1,0:T(8,128)(2,1)}), bf16[8,256,256]{2,1,0:T(8,128)(2,1)}, u32[]{:S(2)}, u32[]{:S(2)}) async-start(bf16[8,256,256]{2,1,0:T(8,128)(2,1)} %bitcast.69), calls=%async_computation.1 | async-start | bytes 2097152 | tf_op jit(solution)/shard_map/all_to_all | solution.py:102
  63.1 12.6 %copy-start.4 = (s32[1,64]{1,0:T(1,128)S(1)}, s32[1,64]{1,0:T(1,128)}, u32[]{:S(2)}) copy-start(s32[1,64]{1,0:T(1,128)} %param.11) | copy-start | bytes 772
  63.2 1.0 copy-start.1
  64.1 1.1 copy-start.2
  65.2 1.1 copy-start.3
  68.5 1.0 copy-start.5
  69.5 1.0 copy-start.7
  70.5 1.0 copy-start.9
  71.5 1.0 copy-start.11
  75.7 1.2 copy-start.6
  76.9 1.2 copy-start.8
  78.2 1.2 copy-start.10
  79.4 1.2 copy-start.12
  92.0 1.0 copy-start.13
  93.0 6.9 %copy-start.14 = (bf16[1024,512]{1,0:T(8,128)(2,1)S(1)}, bf16[1024,512]{1,0:T(8,128)(2,1)}, u32[]{:S(2)}) copy-start(bf16[1024,512]{1,0:T(8,128)(2,1)} %copy-done.13) | copy-start | bytes 3145732
  93.0 19.6 %all-to-all-start.4 = ((bf16[8,256,256]{2,1,0:T(8,128)(2,1)}), bf16[8,256,256]{2,1,0:T(8,128)(2,1)S(1)}, u32[]{:S(2)}, u32[]{:S(2)}) async-start(bf16[8,256,256]{2,1,0:T(8,128)(2,1)} %bitcast.22), calls=%async_computation.4 | async-start | bytes 2097152 | tf_op jit(solution)/shard_map/all_to_all | solution.py:102
  103.2 9.4 %copy-start.15 = (bf16[1280,512]{1,0:T(8,128)(2,1)}, bf16[1280,512]{1,0:T(8,128)(2,1)S(1)}, u32[]{:S(2)}) copy-start(bf16[1280,512]{1,0:T(8,128)(2,1)S(1)} %convolution_convert_fusion) | copy-start | bytes 3932164
  104.2 14.0 %collective-permute-start.5 = (bf16[4,2,80,512]{3,2,1,0:T(8,128)(2,1)}, bf16[4,2,80,512]{3,2,1,0:T(8,128)(2,1)S(1)}, u32[]{:S(2)}, u32[]{:S(2)}) collective-permute-start(bf16[4,2,80,512]{3,2,1,0:T(8,128)(2,1)} %dynamic-slice_bitcast_fusion), channel_id=1, source_target_pairs={{0,32},{2,226},{4,36},{6,230},{8,40},{10,234},{12,44},{14,238},{16... | collective-permute-start | bytes 1966088 | tf_op jit(solution)/shard_map/ppermute | solution.py:98
  112.6 19.5 %all-to-all-start.3 = ((bf16[8,256,256]{2,1,0:T(8,128)(2,1)}), bf16[8,256,256]{2,1,0:T(8,128)(2,1)S(1)}, u32[]{:S(2)}, u32[]{:S(2)}) async-start(bf16[8,256,256]{2,1,0:T(8,128)(2,1)} %bitcast.20), calls=%async_computation.3 | async-start | bytes 2097152 | tf_op jit(solution)/shard_map/all_to_all | solution.py:102
  119.5 11.4 %collective-permute-start.6 = (bf16[4,80,512]{2,1,0:T(8,128)(2,1)S(1)}, bf16[4,80,512]{2,1,0:T(8,128)(2,1)S(1)}, u32[]{:S(2)}, u32[]{:S(2)}) collective-permute-start(bf16[4,80,512]{2,1,0:T(8,128)(2,1)S(1)} %dynamic-slice_bitcast_fusion.1), channel_id=1, source_target_pairs={{0,16},{16,0},{32,48},{48,32},{64,80},{80,64},{96,112},{112,96},{1... | collective-permute-start | bytes 983048 | tf_op jit(solution)/shard_map/ppermute | solution.py:98
  132.1 20.0 %all-to-all-start.5 = ((bf16[4,80,512]{2,1,0:T(8,128)(2,1)}), bf16[4,80,512]{2,1,0:T(8,128)(2,1)S(1)}, u32[]{:S(2)}, u32[]{:S(2)}) async-start(bf16[4,80,512]{2,1,0:T(8,128)(2,1)} %fusion.1), calls=%async_computation.5 | async-start | bytes 655360 | tf_op jit(solution)/shard_map/all_to_all | solution.py:102
